TPU v7x, 32 devices: a whole 2x2x4 slice. The times are simulated.
32 devices in a mesh: dp: 4 (over z), pocket: 8 (over y, x, core).
Axes of the slice: x: 2, y: 2, z: 4, core: 2. Of those that a mesh axis runs over, the one named last changes fastest.
Arguments:
- atoms: bfloat16 [256, 128, 768], P(('dp', 'pocket')), may hold values from -6 to 6
- distance_bins: int32 [256, 128, 128], P(('dp', 'pocket')), may hold values from 0 to 31
- bonds: int32 [256, 128, 128], P(('dp', 'pocket')), may hold values 0 or 1
- molecule: int32 [256, 128], P(('dp', 'pocket')), may hold values from 0 to 3, never falling along the last dimension, each value on 1 to 64 neighbouring positions
- block_counts: int32 [4, 8], P('dp', 'pocket'), may hold values from 1 to 8, as said below
- block_scaffold: int32 [256], replicated, may hold values from 0 to 8191
- pocket_ids: int32 [8192, 4], replicated, may hold values from 0 to 7, as said below
- pocket_keys: bfloat16 [1024, 768], P('pocket'), may hold values from -6 to 6
- pocket_values: bfloat16 [1024, 768], P('pocket'), may hold values from -6 to 6
- pocket_bias: bfloat16 [12, 1024], P(None, 'pocket'), may hold values from -4 to 320
- bin_table: float32 [12, 32], replicated, may hold values from -4 to 320
- bond_weight: float32 [12], replicated, may hold values from 0.5 to 2.5
- w_query: bfloat16 [768, 768], replicated, may hold values from -0.21875 to 0.21875
- w_key: bfloat16 [768, 768], replicated, may hold values from -0.21875 to 0.21875
- w_value: bfloat16 [768, 768], replicated, may hold values from -0.21875 to 0.21875
- w_out: bfloat16 [768, 768], replicated, may hold values from -0.21875 to 0.21875
- w_cross_query: bfloat16 [768, 768], replicated, may hold values from -0.21875 to 0.21875
- w_cross_out: bfloat16 [768, 768], replicated, may hold values from -0.21875 to 0.21875
- cotangent: bfloat16 [128, 128, 768], P(('dp', 'pocket')), may hold values from -6 to 6
Outputs:
- updated: bfloat16 [128, 128, 768], P(('dp', 'pocket'))
- weight_grads: bfloat16 [6, 768, 768], replicated
Inputs may be any that keep to these rules, and one draw needn't show every extreme that they name: `block_counts`: every column sums to 16, and in every column one device has exactly 8 live blocks. `pocket_ids`: each row names 4 different pocket blocks.
All inputs are finite; a program needn't handle non-finite values. No bound on the sum of `bonds` on one device may be relied on, other than what follows from the above.
Results may differ from a plain program's by a relative error of at most 0.012.
The roundings to bfloat16 on the way count: a program that leaves them out, or rounds other values in their place, can miss the bound.
Values may be sent and summed in bfloat16 or wider, within the bound.
A program may use at most 128 MiB of HBM per device.

v0:
```python
import math

import jax
import jax.numpy as jnp
from jax import lax
from jax.sharding import PartitionSpec as P

masked_value = -30000.0


def pair_bias(bin_rows, bond_rows, molecule_rows, bin_table, bond_weight):
    bin_count = bin_table.shape[1]
    levels = lax.broadcasted_iota(jnp.int32, (1, 1, 1, bin_count), 3)
    one_hot = (bin_rows[..., None] == levels).astype(jnp.float32)
    looked_up = jnp.einsum("cijn,hn->chij", one_hot, bin_table, precision=lax.Precision.HIGHEST)
    bonded = looked_up + bond_weight[None, :, None, None] * bond_rows[:, None, :, :].astype(
        jnp.float32
    )
    same_molecule = molecule_rows[:, None, :, None] == molecule_rows[:, None, None, :]
    return jnp.where(same_molecule, bonded, masked_value).astype(jnp.bfloat16)


def project_rows(left, weight):
    flat = left.reshape(-1, left.shape[-1])
    result = jnp.dot(flat, weight, preferred_element_type=jnp.float32)
    return result.reshape(left.shape[:-1] + (weight.shape[1],))


def project_back(left, weight):
    flat = left.reshape(-1, left.shape[-1])
    result = lax.dot_general(
        flat, weight, (((1,), (1,)), ((), ())), preferred_element_type=jnp.float32
    )
    return result.reshape(left.shape[:-1] + (weight.shape[0],))


def weight_product(left, right):
    return lax.dot_general(
        left.reshape(-1, left.shape[-1]),
        right.reshape(-1, right.shape[-1]),
        (((0,), (0,)), ((), ())),
        preferred_element_type=jnp.float32,
    )


def softmax_rows(scores):
    highest = jnp.max(scores, axis=-1, keepdims=True)
    expsum = jnp.exp(scores - highest)
    return expsum / jnp.sum(expsum, axis=-1, keepdims=True)


def split_heads(matrix, heads):
    return matrix.reshape(matrix.shape[0], matrix.shape[1], heads, matrix.shape[2] // heads)


def einsum_mixed(form, left, right):
    return jnp.einsum(form, left, right, preferred_element_type=jnp.float32)


def layer_pass(
    block_atoms, block_bias, cross_keys, cross_values, cross_bias, cotangent_rows, weights, heads
):
    w_query, w_key, w_value, w_out, w_cquery, w_cout = weights
    block_count, row_count, width = block_atoms.shape
    scale = 1.0 / math.sqrt(width // heads)
    query_rows = project_rows(block_atoms, w_query).astype(jnp.bfloat16)
    key_rows = project_rows(block_atoms, w_key).astype(jnp.bfloat16)
    value_rows = project_rows(block_atoms, w_value).astype(jnp.bfloat16)
    query_heads = split_heads(query_rows, heads)
    key_heads = split_heads(key_rows, heads)
    value_heads = split_heads(value_rows, heads)
    scores = einsum_mixed("bihd,bjhd->bhij", query_heads, key_heads) * scale + block_bias.astype(
        jnp.float32
    )
    probs = softmax_rows(scores)
    probs_rounded = probs.astype(jnp.bfloat16)
    attended = (
        einsum_mixed("bhij,bjhd->bihd", probs_rounded, value_heads)
        .reshape(block_count, row_count, width)
        .astype(jnp.bfloat16)
    )
    middle = (block_atoms.astype(jnp.float32) + project_rows(attended, w_out)).astype(jnp.bfloat16)
    cross_query = project_rows(middle, w_cquery).astype(jnp.bfloat16)
    cquery_heads = split_heads(cross_query, heads)
    ckey_heads = split_heads(cross_keys, heads)
    cvalue_heads = split_heads(cross_values, heads)
    cross_scores = (
        einsum_mixed("bihd,bthd->bhit", cquery_heads, ckey_heads) * scale
        + cross_bias.astype(jnp.float32)[:, :, None, :]
    )
    cross_probs = softmax_rows(cross_scores)
    cross_rounded = cross_probs.astype(jnp.bfloat16)
    cross_attended = (
        einsum_mixed("bhit,bthd->bihd", cross_rounded, cvalue_heads)
        .reshape(block_count, row_count, width)
        .astype(jnp.bfloat16)
    )
    updated = (middle.astype(jnp.float32) + project_rows(cross_attended, w_cout)).astype(
        jnp.bfloat16
    )
    grad_cout = weight_product(cross_attended, cotangent_rows)
    d_cross = project_back(cotangent_rows, w_cout).astype(jnp.bfloat16)
    d_cross_probs = einsum_mixed("bihd,bthd->bhit", split_heads(d_cross, heads), cvalue_heads)
    d_cross_scores = (
        cross_probs
        * (d_cross_probs - jnp.sum(cross_probs * d_cross_probs, axis=-1, keepdims=True))
        * scale
    ).astype(jnp.bfloat16)
    d_cross_query = (
        einsum_mixed("bhit,bthd->bihd", d_cross_scores, ckey_heads)
        .reshape(block_count, row_count, width)
        .astype(jnp.bfloat16)
    )
    grad_cquery = weight_product(middle, d_cross_query)
    d_middle = (cotangent_rows.astype(jnp.float32) + project_back(d_cross_query, w_cquery)).astype(
        jnp.bfloat16
    )
    grad_out = weight_product(attended, d_middle)
    d_attended = project_back(d_middle, w_out).astype(jnp.bfloat16)
    dattn_heads = split_heads(d_attended, heads)
    d_probs = einsum_mixed("bihd,bjhd->bhij", dattn_heads, value_heads)
    d_scores = (
        probs * (d_probs - jnp.sum(probs * d_probs, axis=-1, keepdims=True)) * scale
    ).astype(jnp.bfloat16)
    d_query = (
        einsum_mixed("bhij,bjhd->bihd", d_scores, key_heads)
        .reshape(block_count, row_count, width)
        .astype(jnp.bfloat16)
    )
    d_key = (
        einsum_mixed("bhij,bihd->bjhd", d_scores, query_heads)
        .reshape(block_count, row_count, width)
        .astype(jnp.bfloat16)
    )
    d_value = (
        einsum_mixed("bhij,bihd->bjhd", probs_rounded, dattn_heads)
        .reshape(block_count, row_count, width)
        .astype(jnp.bfloat16)
    )
    grad_query = weight_product(block_atoms, d_query)
    grad_key = weight_product(block_atoms, d_key)
    grad_value = weight_product(block_atoms, d_value)
    grads = jnp.stack([grad_query, grad_key, grad_value, grad_out, grad_cquery, grad_cout])
    return (updated, grads)


def on_device(
    atoms,
    distance_bins,
    bonds,
    molecule,
    block_counts,
    block_scaffold,
    pocket_ids,
    pocket_keys,
    pocket_values,
    pocket_bias,
    bin_table,
    bond_weight,
    w_query,
    w_key,
    w_value,
    w_out,
    w_cross_query,
    w_cross_out,
    cotangent,
):
    dp_count = lax.axis_size("dp")
    pocket_count = lax.axis_size("pocket")
    capacity = atoms.shape[0]
    balanced = cotangent.shape[0]
    row_count = atoms.shape[1]
    width = atoms.shape[2]
    heads = bin_table.shape[0]
    per_target = capacity // dp_count
    counts = lax.all_gather(block_counts.reshape(1), "dp", axis=0, tiled=True)
    offsets = jnp.cumsum(counts) - counts
    own_device = lax.axis_index("dp")
    own_column = lax.axis_index("pocket")
    own_offset = offsets[own_device]
    own_count = counts[own_device]
    target_rows = lax.broadcasted_iota(jnp.int32, (dp_count, per_target), 0)
    turn_index = lax.broadcasted_iota(jnp.int32, (dp_count, per_target), 1)
    outgoing = jnp.mod(target_rows - own_offset, dp_count) + dp_count * turn_index
    picked = jnp.where(outgoing < own_count, outgoing, 0).reshape(-1)
    source_offset = offsets[:, None]
    source_count = counts[:, None]
    incoming = jnp.mod(own_device - source_offset, dp_count) + dp_count * turn_index
    usable = incoming < source_count
    landing = (source_offset + incoming) // dp_count
    wanted = lax.broadcasted_iota(jnp.int32, (balanced, 1), 0)
    matches = (landing.reshape(1, -1) == wanted) & usable.reshape(1, -1)
    received_index = lax.broadcasted_iota(jnp.int32, (balanced, dp_count * per_target), 1)
    position = jnp.sum(jnp.where(matches, received_index, 0), axis=1)
    local_bias = pair_bias(distance_bins, bonds, molecule, bin_table, bond_weight)
    got_atoms, got_bias = (
        lax.all_to_all(atoms[picked], "dp", split_axis=0, concat_axis=0, tiled=True),
        lax.all_to_all(local_bias[picked], "dp", split_axis=0, concat_axis=0, tiled=True),
    )
    block_atoms = got_atoms[position]
    block_bias = got_bias[position]
    anchor = ((target_rows * pocket_count + own_column) * capacity + incoming).reshape(-1)[position]
    scaffold = block_scaffold[anchor]
    all_keys, all_values, all_bias = (
        lax.all_gather(pocket_keys, "pocket", axis=0, tiled=True),
        lax.all_gather(pocket_values, "pocket", axis=0, tiled=True),
        lax.all_gather(pocket_bias, "pocket", axis=1, tiled=True),
    )
    pocket_blocks = all_keys.shape[0] // row_count
    chosen = pocket_ids[scaffold]
    cross_keys = all_keys.reshape(pocket_blocks, row_count, width)[chosen].reshape(
        balanced, -1, width
    )
    cross_values = all_values.reshape(pocket_blocks, row_count, width)[chosen].reshape(
        balanced, -1, width
    )
    cross_bias = jnp.transpose(
        all_bias.reshape(heads, pocket_blocks, row_count)[:, chosen], (1, 0, 2, 3)
    ).reshape(balanced, heads, -1)
    per_pass = math.gcd(balanced, max(1, 512 // row_count))
    passes = balanced // per_pass
    weights = (w_query, w_key, w_value, w_out, w_cross_query, w_cross_out)

    def regroup(matrix):
        return matrix.reshape((passes, per_pass) + matrix.shape[1:])

    def one_pass(total, inputs):
        pass_atoms, pass_bias, pass_keys, pass_values, pass_cross_bias, pass_cotangent = inputs
        updated_rows, grads = layer_pass(
            pass_atoms,
            pass_bias,
            pass_keys,
            pass_values,
            pass_cross_bias,
            pass_cotangent,
            weights,
            heads,
        )
        return (total + grads, updated_rows)

    start_total = jnp.zeros((6, width, width), jnp.float32)
    total, updated = lax.scan(
        one_pass,
        start_total,
        (
            regroup(block_atoms),
            regroup(block_bias),
            regroup(cross_keys),
            regroup(cross_values),
            regroup(cross_bias),
            regroup(cotangent),
        ),
    )
    updated = updated.reshape(cotangent.shape)
    scale = 1.0 / math.sqrt(balanced * row_count * dp_count * pocket_count)
    weight_grads = (lax.psum(total, ("dp", "pocket")) * scale).astype(jnp.bfloat16)
    return (updated, weight_grads)


def solution(mesh):
    return jax.shard_map(
        on_device,
        mesh=mesh,
        in_specs=(
            P(("dp", "pocket"), None, None),
            P(("dp", "pocket"), None, None),
            P(("dp", "pocket"), None, None),
            P(("dp", "pocket"), None),
            P("dp", "pocket"),
            P(),
            P(),
            P("pocket", None),
            P("pocket", None),
            P(None, "pocket"),
            P(),
            P(),
            P(),
            P(),
            P(),
            P(),
            P(),
            P(),
            P(("dp", "pocket"), None, None),
        ),
        out_specs=(P(("dp", "pocket"), None, None), P()),
        check_vma=False,
    )
```

profile of v0, /device:TPU:0, one launch (start us, length us, event | category | flops | bytes accessed | tf_op | source)
XLA Modules:
  0.0 522.3 jit_solution(13700364734158510550)
XLA Ops:
  9.9 9.9 %all-reduce = s32[4]{0:T(128)S(1)} all-reduce(s32[4]{0:T(128)S(1)} %bitcast_dynamic-update-slice_fusion.6), channel_id=2, replica_groups=mesh['dp'=4,'pocket'=8] {'dp'}, use_global_device_ids=true, to_apply=%add | all-reduce | flops 4 | bytes 32 | tf_op jit(solution)/shard_map/all_gather | solution.py:176
  27.2 3.7 all-to-all-start
  31.9 7.7 %fusion.8 = bf16[8,12,128,128]{3,1,2,0:T(8,128)(2,1)} fusion(f32[8,128,128]{2,1,0:T(8,128)S(1)} %convert_element_type.163, f32[12]{0:T(128)S(1)} %copy-done.26, pred[8,128,128]{2,1,0:T(8,128)(4,1)S(1)} %broadcast_compare_fusion, s32[8,128,128]{2,1,0:T(8,128)S(1)} %copy-done.24, f32[12,32]{1,0:T(8,128)S(1)} %copy-done.25), kind=kOutput, calls=%fused_computation.25 | convolution fusion | flops 614465536 | bytes 4326960 | tf_op jit(solution)/shard_map/cijn,hn->chij/dot_general | solution.py:15
  39.6 5.3 %gather_fusion.2 = bf16[8,12,128,128]{3,1,2,0:T(8,128)(2,1)} fusion(bf16[8,12,128,128]{3,1,2,0:T(8,128)(2,1)} %fusion.8, s32[1024]{0:T(1024)S(1)} %get-tuple-element.41), kind=kCustom, calls=%fused_computation.2 | custom fusion | bytes 6291488 | tf_op jit(solution)/shard_map/gather | solution.py:198
  44.9 4.7 copy.147
  49.6 16.4 %all-to-all-done = bf16[8,128,768]{2,1,0:T(8,128)(2,1)S(1)} async-done(((bf16[8,128,768]{2,1,0:T(8,128)(2,1)}), bf16[8,128,768]{2,1,0:T(8,128)(2,1)S(1)}, u32[]{:S(2)}, u32[]{:S(2)}) %all-to-all-start) | async-done | bytes 1572896 | tf_op jit(solution)/shard_map/all_to_all | solution.py:197
  66.1 4.7 all-to-all-start.1
  77.1 8.9 %all_gather.15 = bf16[12,1024]{1,0:T(8,128)(2,1)S(1)} all-gather(bf16[12,128]{1,0:T(8,128)(2,1)S(1)} %copy-done.22), channel_id=1, replica_groups=mesh['dp'=4,'pocket'=8] {'pocket'}, dimensions={1}, use_global_device_ids=true | all-gather | bytes 27648 | tf_op jit(solution)/shard_map/all_gather | solution.py:207
  101.5 3.8 gather_fusion.7
  105.3 5.3 %copy.152 = bf16[16,128,768]{1,0,2:T(8,128)(2,1)} copy(bf16[16,128,768]{2,1,0:T(8,128)(2,1)} %gather_fusion.7) | data formatting | bytes 6291456 | tf_op jit(solution)/shard_map/gather | solution.py:214
  110.5 5.7 %reshape.416 = bf16[4,512,12,64]{1,0,3,2:T(4,128)(2,1)} reshape(bf16[16,128,768]{1,0,2:T(8,128)(2,1)} %copy.152) | data formatting | bytes 6291456 | tf_op jit(solution)/shard_map/while/body/eval_jaxpr/reshape | solution.py:53
  116.2 3.8 gather_fusion.8
  120.1 5.1 copy.154
  125.2 5.7 %reshape.419 = bf16[4,512,12,64]{1,0,3,2:T(4,128)(2,1)} reshape(bf16[16,128,768]{1,0,2:T(8,128)(2,1)} %copy.154) | data formatting | bytes 6291456 | tf_op jit(solution)/shard_map/while/body/eval_jaxpr/reshape | solution.py:53
  130.9 8.2 %fusion.21 = f32[4,12,128,512]{3,2,1,0:T(8,128)} fusion(bf16[4,128,12,64]{1,3,2,0:T(8,128)(2,1)S(1)} %bitcast.153, bf16[4,512,12,64]{1,0,3,2:T(4,128)(2,1)} %reshape.416), kind=kOutput, calls=%fused_computation.39 | convolution fusion | flops 402653184 | bytes 16515072 | tf_op jit(solution)/shard_map/while/body/eval_jaxpr/bihd,bthd->bhit/dot_general | solution.py:57
  145.3 4.7 fusion.85
  157.2 3.7 fusion.25
  161.0 6.6 %fusion.86 = (f32[4,12,128]{2,1,0:T(8,128)S(1)}, f32[4,12,128,512]{3,2,1,0:T(8,128)}) fusion(f32[4,12,128,512]{3,2,1,0:T(8,128)S(1)} %fusion.25, f32[4,12,512]{2,1,0:T(8,128)S(1)} %copy.158), kind=kOutput, calls=%fused_computation.136 | output fusion | flops 18874880 | bytes 25288704 | tf_op jit(solution)/shard_map/while/body/eval_jaxpr/sub | solution.py:48
  167.6 9.1 %fusion.50 = bf16[4,12,64,128]{3,2,1,0:T(8,128)(2,1)} fusion(bf16[4,512,12,64]{1,0,3,2:T(4,128)(2,1)} %reshape.416, f32[4,12,128,512]{3,2,1,0:T(8,128)} %get-tuple-element.39, f32[4,12,128]{2,1,0:T(8,128)S(1)} %get-tuple-element.38), kind=kOutput, calls=%fused_computation.70 | convolution fusion | flops 409337856 | bytes 16539648 | tf_op jit(solution)/shard_map/while/body/eval_jaxpr/bhit,bthd->bihd/dot_general | solution.py:57
  176.7 44.4 %fusion.39 = bf16[4,12,64,128]{3,2,1,0:T(8,128)(2,1)} fusion(f32[4,12,128,512]{3,2,1,0:T(8,128)} %fusion.21, bf16[4,512,12,64]{1,0,3,2:T(4,128)(2,1)} %reshape.419, f32[4,12,128,512]{3,2,1,0:T(8,128)} %get-tuple-element.39, f32[4,12,128]{2,1,0:T(8,128)S(1)} %get-tuple-element.38), kind=kOutput, calls=%fused_computation.61 | convolution fusion | flops 425073152 | bytes 29122560 | tf_op jit(solution)/shard_map/while/body/eval_jaxpr/bhit,bthd->bihd/dot_general | solution.py:57
  230.0 6.9 %fusion.44 = bf16[4,12,64,128]{3,2,1,0:T(8,128)(2,1)} fusion(bf16[4,128,12,64]{1,3,2,0:T(8,128)(2,1)} %bitcast.166, f32[4,12,128,128]{2,3,1,0:T(8,128)} %fusion.87, f32[4,12,128,128]{2,3,1,0:T(8,128)} %get-tuple-element.37, f32[4,12,128]{2,1,0:T(8,128)S(1)} %get-tuple-element.36), kind=kOutput, calls=%fused_computation.68 | convolution fusion | flops 106567808 | bytes 7888896 | tf_op jit(solution)/shard_map/while/body/eval_jaxpr/bhij,bjhd->bihd/dot_general | solution.py:57
  236.9 6.6 %fusion.47 = bf16[4,12,64,128]{3,2,1,0:T(8,128)(2,1)} fusion(bf16[4,128,12,64]{1,3,2,0:T(8,128)(2,1)S(1)} %bitcast.164, f32[4,12,128,128]{2,3,1,0:T(8,128)} %fusion.87, f32[4,12,128,128]{2,3,1,0:T(8,128)} %get-tuple-element.37, f32[4,12,128]{2,1,0:T(8,128)S(1)} %get-tuple-element.36), kind=kOutput, calls=%fused_computation.69 | convolution fusion | flops 106567808 | bytes 7888896 | tf_op jit(solution)/shard_map/while/body/eval_jaxpr/bhij,bihd->bjhd/dot_general | solution.py:57
  263.1 242.9 %all-reduce.3.cloned.1.call-done = f32[6,768,768]{2,1,0:T(8,128)} async-done(((f32[6,768,768]{2,1,0:T(8,128)}), f32[6,768,768]{2,1,0:T(8,128)}) %all-reduce.3.cloned.1.call-update) | async-done | bytes 14155792 | tf_op jit(solution)/shard_map/psum | solution.py:256
  506.0 9.4 %multiply_convert_fusion = bf16[6,768,768]{2,1,0:T(8,128)(2,1)} fusion(f32[6,768,768]{2,1,0:T(8,128)} %all-reduce.3.cloned.1.call-done), kind=kLoop, calls=%fused_computation.16 | loop fusion | flops 7077888 | bytes 21233664 | tf_op jit(solution)/shard_map/convert_element_type | solution.py:256
  (135 shorter events, 73.6 us)
Async XLA Ops:
  7.2 18.1 %copy-start = (bf16[8,128,768]{2,1,0:T(8,128)(2,1)S(1)}, bf16[8,128,768]{2,1,0:T(8,128)(2,1)}, u32[]{:S(2)}) copy-start(bf16[8,128,768]{2,1,0:T(8,128)(2,1)} %param.19) | copy-start | bytes 4718596
  25.3 6.4 %copy-start.21 = (s32[8,128]{1,0:T(8,128)S(1)}, s32[8,128]{1,0:T(8,128)}, u32[]{:S(2)}) copy-start(s32[8,128]{1,0:T(8,128)} %param.22) | copy-start | bytes 12292
  25.3 6.6 %copy-start.25 = (f32[12,32]{1,0:T(8,128)S(1)}, f32[12,32]{1,0:T(8,128)}, u32[]{:S(2)}) copy-start(f32[12,32]{1,0:T(8,128)} %param.29) | copy-start | bytes 4612
  25.3 6.6 %copy-start.26 = (f32[12]{0:T(128)S(1)}, f32[12]{0:T(128)}, u32[]{:S(2)}) copy-start(f32[12]{0:T(128)} %param.30) | copy-start | bytes 148
  27.2 4.4 copy-start.19
  27.2 4.7 copy-start.24
  27.2 38.9 %all-to-all-start = ((bf16[8,128,768]{2,1,0:T(8,128)(2,1)}), bf16[8,128,768]{2,1,0:T(8,128)(2,1)S(1)}, u32[]{:S(2)}, u32[]{:S(2)}) async-start(bf16[8,128,768]{2,1,0:T(8,128)(2,1)} %gather_fusion), calls=%async_computation | async-start | bytes 3145728 | tf_op jit(solution)/shard_map/all_to_all | solution.py:197
  30.9 70.6 %all-gather.4.cloned.1.call-start = ((), (), s32[]{:S(2)}) async-start(), calls=%async_computation.2 | async-start | bytes 1769472 | tf_op jit(solution)/shard_map/all_gather | solution.py:206
  49.6 22.0 %copy-start.20 = (s32[8192,4]{0,1:T(4,128)S(1)}, s32[8192,4]{0,1:T(4,128)}, u32[]{:S(2)}) copy-start(s32[8192,4]{0,1:T(4,128)} %param.25) | copy-start | bytes 393220
  66.1 74.9 %all-to-all-start.1 = ((bf16[8,12,128,128]{3,2,1,0:T(8,128)(2,1)}), bf16[8,12,128,128]{3,2,1,0:T(8,128)(2,1)}, u32[]{:S(2)}, u32[]{:S(2)}) async-start(bf16[8,12,128,128]{3,2,1,0:T(8,128)(2,1)} %copy.147), calls=%async_computation.1 | async-start | bytes 6291456 | tf_op jit(solution)/shard_map/all_to_all | solution.py:198
  70.8 6.4 %copy-start.22 = (bf16[12,128]{1,0:T(8,128)(2,1)S(1)}, bf16[12,128]{1,0:T(8,128)(2,1)}, u32[]{:S(2)}) copy-start(bf16[12,128]{1,0:T(8,128)(2,1)} %param.28) | copy-start | bytes 9220
  70.8 16.0 %copy-start.8 = (bf16[768,768]{1,0:T(8,128)(2,1)S(1)}, bf16[768,768]{1,0:T(8,128)(2,1)}, u32[]{:S(2)}) copy-start(bf16[768,768]{1,0:T(8,128)(2,1)} %param.36) | copy-start | bytes 3538948
  70.8 45.5 %all-gather.6.cloned.1.call-start = ((), (), s32[]{:S(2)}) async-start(), calls=%async_computation.3 | async-start | bytes 1769472 | tf_op jit(solution)/shard_map/all_gather | solution.py:205
  71.5 434.5 %all-reduce.3.cloned.1.call-start = ((), (), s32[]{:S(2)}) async-start(), calls=%async_computation.4 | async-start | bytes 28311552 | tf_op jit(solution)/shard_map/psum | solution.py:256
  139.1 6.2 %copy-start.10 = (bf16[4,128,768]{1,2,0:T(8,128)(2,1)S(1)}, bf16[4,128,768]{1,2,0:T(8,128)(2,1)}, u32[]{:S(2)}) copy-start(bf16[4,128,768]{1,2,0:T(8,128)(2,1)} %copy.145) | copy-start | bytes 2359300
  145.3 4.7 copy-start.2
  176.7 44.4 %copy-start.12 = (bf16[4,128,768]{2,1,0:T(8,128)(2,1)S(1)}, bf16[4,128,768]{2,1,0:T(8,128)(2,1)}, u32[]{:S(2)}) copy-start(bf16[4,128,768]{2,1,0:T(8,128)(2,1)} %param.37) | copy-start | bytes 2359300
  230.0 6.9 %copy-start.11 = (bf16[4,128,768]{1,2,0:T(8,128)(2,1)S(1)}, bf16[4,128,768]{1,2,0:T(8,128)(2,1)}, u32[]{:S(2)}) copy-start(bf16[4,128,768]{1,2,0:T(8,128)(2,1)} %copy.145) | copy-start | bytes 2359300
  248.9 4.5 copy-start.5
  248.9 4.5 copy-start.16
  251.1 4.5 copy-start.14
  253.4 4.5 copy-start.3
  253.4 4.5 copy-start.13
  506.0 9.4 %copy-start.1 = (bf16[8,128,768]{2,1,0:T(8,128)(2,1)S(1)}, bf16[8,128,768]{2,1,0:T(8,128)(2,1)}, u32[]{:S(2)}) copy-start(bf16[8,128,768]{2,1,0:T(8,128)(2,1)} %param.19) | copy-start | bytes 4718596
  (8 other events, 16.0 us)
Sparse Core Ops, SparseCore 0:
  33.6 27.1 all-gather.3
  73.5 27.1 all-gather.5
  260.3 245.6 all-reduce.2
where the time goes:
time: 531 us; the launch traced here: 522 us
  waiting for transfers between devices  263 us (50%)
  matrix products  130 us (24%)
  local copies, waits for them, and re-layouts  68.9 us (13%)
  blocking collectives  18.8 us (4%)
  other arithmetic  18 us (3%)
  between operations  15.4 us (3%)
  starting transfers between devices  8.5 us (2%)
    psum x1, waiting for transfers between devices, on_device(): lax.psum(total, ('dp', 'pocket')) * scale  243 us
    dot_general x9, matrix products, einsum_mixed(): return jnp.einsum(form, left, right, preferred_element_type=jnp.float32)  87 us
    all_to_all x1, waiting for transfers between devices, on_device(): lax.all_to_all(atoms[picked], 'dp', split_axis=0, concat_axis=0, tiled=True)  16.4 us
    dot_general x6, matrix products, weight_product(): lax.dot_general(left.reshape(-1, left.shape[-1]), right.reshape(-1, right...  13.5 us
    reshape x2, local copies, waits for them, and re-layouts, split_heads(): matrix.reshape(matrix.shape[0], matrix.shape[1], heads, matrix.shape[2] /...  11.4 us
  transfers between devices with their start and end apart: 5, of which 3 were waited for; matrix products, arithmetic and copies ran while one was open for 15% of the time, Pallas kernels for 0%

commit v1 on v0

--- a/solution.py
+++ b/solution.py
@@ -142,6 +142,11 @@
     grad_value = weight_product(block_atoms, d_value)
     grads = jnp.stack([grad_query, grad_key, grad_value, grad_out, grad_cquery, grad_cout])
     return (updated, grads)
+
+
+def pick(array, index):
+    rows = [lax.dynamic_slice_in_dim(array, index[i], 1, 0) for i in range(index.shape[0])]
+    return jnp.concatenate(rows, axis=0)
 
 
 def on_device(
@@ -174,7 +179,9 @@
     heads = bin_table.shape[0]
     per_target = capacity // dp_count
     counts = lax.all_gather(block_counts.reshape(1), "dp", axis=0, tiled=True)
-    offsets = jnp.cumsum(counts) - counts
+    places = lax.broadcasted_iota(jnp.int32, (dp_count, dp_count), 0)
+    before = places > lax.broadcasted_iota(jnp.int32, (dp_count, dp_count), 1)
+    offsets = jnp.sum(jnp.where(before, counts[None, :], 0), axis=1)
     own_device = lax.axis_index("dp")
     own_column = lax.axis_index("pocket")
     own_offset = offsets[own_device]
@@ -194,28 +201,33 @@
     position = jnp.sum(jnp.where(matches, received_index, 0), axis=1)
     local_bias = pair_bias(distance_bins, bonds, molecule, bin_table, bond_weight)
     got_atoms, got_bias = (
-        lax.all_to_all(atoms[picked], "dp", split_axis=0, concat_axis=0, tiled=True),
-        lax.all_to_all(local_bias[picked], "dp", split_axis=0, concat_axis=0, tiled=True),
-    )
-    block_atoms = got_atoms[position]
-    block_bias = got_bias[position]
-    anchor = ((target_rows * pocket_count + own_column) * capacity + incoming).reshape(-1)[position]
-    scaffold = block_scaffold[anchor]
+        lax.all_to_all(pick(atoms, picked), "dp", split_axis=0, concat_axis=0, tiled=True),
+        lax.all_to_all(pick(local_bias, picked), "dp", split_axis=0, concat_axis=0, tiled=True),
+    )
+    block_atoms = pick(got_atoms, position)
+    block_bias = pick(got_bias, position)
+    anchor = ((target_rows * pocket_count + own_column) * capacity + incoming).reshape(-1)
+    anchor = pick(anchor, position)
+    scaffold = pick(block_scaffold, anchor)
     all_keys, all_values, all_bias = (
         lax.all_gather(pocket_keys, "pocket", axis=0, tiled=True),
         lax.all_gather(pocket_values, "pocket", axis=0, tiled=True),
         lax.all_gather(pocket_bias, "pocket", axis=1, tiled=True),
     )
     pocket_blocks = all_keys.shape[0] // row_count
-    chosen = pocket_ids[scaffold]
-    cross_keys = all_keys.reshape(pocket_blocks, row_count, width)[chosen].reshape(
+    chosen = pick(pocket_ids, scaffold)
+    flat_chosen = chosen.reshape(-1)
+    cross_keys = pick(all_keys.reshape(pocket_blocks, row_count, width), flat_chosen).reshape(
         balanced, -1, width
     )
-    cross_values = all_values.reshape(pocket_blocks, row_count, width)[chosen].reshape(
+    cross_values = pick(all_values.reshape(pocket_blocks, row_count, width), flat_chosen).reshape(
         balanced, -1, width
     )
     cross_bias = jnp.transpose(
-        all_bias.reshape(heads, pocket_blocks, row_count)[:, chosen], (1, 0, 2, 3)
+        pick(
+            jnp.transpose(all_bias.reshape(heads, pocket_blocks, row_count), (1, 0, 2)), flat_chosen
+        ).reshape(chosen.shape + (heads, row_count)),
+        (0, 2, 1, 3),
     ).reshape(balanced, heads, -1)
     per_pass = math.gcd(balanced, max(1, 512 // row_count))
     passes = balanced // per_pass

time: 531 us -> 706 us (1.33)
  local copies, waits for them, and re-layouts: 68.9 us -> 170 us
  between operations: 15.4 us -> 82.9 us
  waiting for transfers between devices: 263 us -> 251 us
    unnamed x60 -> x123, local copies, waits for them, and re-layouts: 8.17 us -> 79.4 us
    concatenate x0 -> x6, local copies, waits for them, and re-layouts: none -> 41.5 us  [pick(): return jnp.concatenate(rows, axis=0)]
    gather x14 -> x0, local copies, waits for them, and re-layouts: 40 us -> none  [the longest x2 9.98 us: on_device(): local_bias[picked]]
    dynamic_slice x0 -> x8, local copies, waits for them, and re-layouts: none -> 14.2 us  [pick(): lax.dynamic_slice_in_dim(array, index[i], 1, 0)]
    all_to_all x2, waiting for transfers between devices: 18.3 us -> 4.99 us  [the longest x1 4.99 us: on_device(): lax.all_to_all(pick(atoms, picked), 'dp', split_axis=0, concat_axis=0, ti...]
    dot_general x0 -> x1, local copies, waits for them, and re-layouts: none -> 8.49 us  [pair_bias(): jnp.einsum('cijn,hn->chij', one_hot, bin_table, precision=lax.Precision.H...]
  transfers between devices with their start and end apart: 5 -> 5, of which waited for: 3 -> 2; matrix products, arithmetic and copies ran while one was open for 15% -> 26% of each run, Pallas kernels for 0% -> 0%
where the time goes in v1:
time: 706 us; the launch traced here: 693 us
  waiting for transfers between devices  251 us (36%)
  local copies, waits for them, and re-layouts  170 us (24%)
  matrix products  137 us (19%)
  between operations  82.9 us (12%)
  other arithmetic  25 us (4%)
  blocking collectives  19 us (3%)
  starting transfers between devices  8.4 us (1%)
    psum x1, waiting for transfers between devices, on_device(): lax.psum(total, ('dp', 'pocket')) * scale  244 us
    dot_general x9, matrix products, einsum_mixed(): return jnp.einsum(form, left, right, preferred_element_type=jnp.float32)  89.9 us
    unnamed x123, local copies, waits for them, and re-layouts  79.4 us
    concatenate x6, local copies, waits for them, and re-layouts, pick(): return jnp.concatenate(rows, axis=0)  41.5 us
    dot_general x6, matrix products, weight_product(): lax.dot_general(left.reshape(-1, left.shape[-1]), right.reshape(-1, right...  14.7 us
    dynamic_slice x8, local copies, waits for them, and re-layouts, pick(): lax.dynamic_slice_in_dim(array, index[i], 1, 0)  14.2 us
  transfers between devices with their start and end apart: 5, of which 2 were waited for; matrix products, arithmetic and copies ran while one was open for 26% of the time, Pallas kernels for 0%

profile of v1, /device:TPU:0, one launch (start us, length us, event | category | flops | bytes accessed | tf_op | source)
XLA Modules:
  0.0 693.2 jit_solution(8772464889040053362)
XLA Ops:
  9.9 9.9 %all-reduce = s32[4]{0:T(128)S(1)} all-reduce(s32[4]{0:T(128)S(1)} %bitcast_dynamic-update-slice_fusion.6), channel_id=2, replica_groups=mesh['dp'=4,'pocket'=8] {'dp'}, use_global_device_ids=true, to_apply=%add | all-reduce | flops 4 | bytes 32 | tf_op jit(solution)/shard_map/all_gather | solution.py:181
  67.0 8.2 %fusion.4 = f32[8,128,128,12]{2,3,1,0:T(8,128)} fusion(s32[8,128,128]{2,1,0:T(8,128)} %param.20, f32[12,32]{1,0:T(8,128)S(1)} %copy-done.28), kind=kOutput, calls=%fused_computation.5 | convolution fusion | flops 608174080 | bytes 6817280 | tf_op jit(solution)/shard_map/cijn,hn->chij/dot_general | solution.py:15
  75.2 8.5 %copy.238 = f32[8,128,128,12]{1,2,3,0:T(8,128)} copy(f32[8,128,128,12]{2,3,1,0:T(8,128)} %fusion.4) | data formatting | bytes 12582912 | tf_op jit(solution)/shard_map/cijn,hn->chij/dot_general | solution.py:15
  83.9 4.2 fusion.14
  94.3 5.0 all-to-all-done
  99.3 4.7 all-to-all-start.1
  142.3 9.1 %all_gather.15 = bf16[12,1024]{1,0:T(8,128)(2,1)S(1)} all-gather(bf16[12,128]{1,0:T(8,128)(2,1)S(1)} %copy-done.29), channel_id=1, replica_groups=mesh['dp'=4,'pocket'=8] {'pocket'}, dimensions={1}, use_global_device_ids=true | all-gather | bytes 27648 | tf_op jit(solution)/shard_map/all_gather | solution.py:215
  186.8 3.6 constant_dynamic-slice_fusion.16
  219.2 18.0 %concatenate.30 = bf16[16,128,768]{1,0,2:T(8,128)(2,1)} concatenate(bf16[1,128,768]{1,0,2:T(2,128)(2,1)} %copy.344, bf16[1,128,768]{1,0,2:T(2,128)(2,1)} %copy.345, bf16[1,128,768]{1,0,2:T(2,128)(2,1)} %copy.346, bf16[1,128,768]{1,0,2:T(2,128)(2,1)} %copy.347, bf16[1,128,768]{1,0,2:T(2,128)(2,1)} %copy.348, bf16[1,128,768]{1,0,2:T(2,128)(2,1)} %copy.349, ...), dimensions={0} | concatenate | bytes 6291456 | tf_op jit(solution)/shard_map/concatenate | solution.py:149
  237.2 5.7 reshape.295
  242.9 3.6 constant_dynamic-slice_fusion.32
  275.2 18.0 %concatenate.29 = bf16[16,128,768]{1,0,2:T(8,128)(2,1)} concatenate(bf16[1,128,768]{1,0,2:T(2,128)(2,1)} %copy.328, bf16[1,128,768]{1,0,2:T(2,128)(2,1)} %copy.329, bf16[1,128,768]{1,0,2:T(2,128)(2,1)} %copy.330, bf16[1,128,768]{1,0,2:T(2,128)(2,1)} %copy.331, bf16[1,128,768]{1,0,2:T(2,128)(2,1)} %copy.332, bf16[1,128,768]{1,0,2:T(2,128)(2,1)} %copy.333, ...), dimensions={0} | concatenate | bytes 6291456 | tf_op jit(solution)/shard_map/concatenate | solution.py:149
  293.2 6.1 reshape.292
  299.4 8.2 %fusion.21 = f32[4,12,128,512]{3,2,1,0:T(8,128)} fusion(bf16[4,128,12,64]{1,3,2,0:T(8,128)(2,1)S(1)} %bitcast.194, bf16[4,512,12,64]{1,0,3,2:T(4,128)(2,1)} %reshape.292), kind=kOutput, calls=%fused_computation.29 | convolution fusion | flops 402653184 | bytes 16515072 | tf_op jit(solution)/shard_map/while/body/eval_jaxpr/bihd,bthd->bhit/dot_general | solution.py:57
  310.3 4.9 fusion.103
  321.9 3.7 fusion.25
  325.6 7.4 %fusion.104 = (f32[4,12,128]{2,1,0:T(8,128)S(1)}, f32[4,12,128,512]{3,2,1,0:T(8,128)}) fusion(f32[4,12,128,512]{3,2,1,0:T(8,128)S(1)} %fusion.25, f32[4,12,512]{2,1,0:T(8,128)} %copy.293), kind=kOutput, calls=%fused_computation.212 | output fusion | flops 18874880 | bytes 25288704 | tf_op jit(solution)/shard_map/while/body/eval_jaxpr/sub | solution.py:48
  333.6 9.2 %fusion.50 = bf16[4,12,64,128]{3,2,1,0:T(8,128)(2,1)} fusion(bf16[4,512,12,64]{1,0,3,2:T(4,128)(2,1)} %reshape.292, f32[4,12,128,512]{3,2,1,0:T(8,128)} %get-tuple-element.149, f32[4,12,128]{2,1,0:T(8,128)S(1)} %get-tuple-element.148), kind=kOutput, calls=%fused_computation.61 | convolution fusion | flops 409337856 | bytes 16539648 | tf_op jit(solution)/shard_map/while/body/eval_jaxpr/bhit,bthd->bihd/dot_general | solution.py:57
  342.8 46.4 %fusion.39 = bf16[4,12,64,128]{3,2,1,0:T(8,128)(2,1)} fusion(f32[4,12,128,512]{3,2,1,0:T(8,128)} %fusion.21, bf16[4,512,12,64]{1,0,3,2:T(4,128)(2,1)} %reshape.295, f32[4,12,128,512]{3,2,1,0:T(8,128)} %get-tuple-element.149, f32[4,12,128]{2,1,0:T(8,128)} %copy-done.26), kind=kOutput, calls=%fused_computation.52 | convolution fusion | flops 425073152 | bytes 29122560 | tf_op jit(solution)/shard_map/while/body/eval_jaxpr/bhit,bthd->bihd/dot_general | solution.py:57
  395.4 4.0 convolution_convert_fusion.6
  401.6 6.9 fusion.44
  408.5 6.7 fusion.47
  433.0 244.3 %all-reduce.3.cloned.1.call-done = f32[6,768,768]{2,1,0:T(8,128)} async-done(((f32[6,768,768]{2,1,0:T(8,128)}), f32[6,768,768]{2,1,0:T(8,128)}) %all-reduce.3.cloned.1.call-update) | async-done | bytes 14155792 | tf_op jit(solution)/shard_map/psum | solution.py:268
  677.3 9.2 %multiply_convert_fusion = bf16[6,768,768]{2,1,0:T(8,128)(2,1)} fusion(f32[6,768,768]{2,1,0:T(8,128)} %all-reduce.3.cloned.1.call-done), kind=kLoop, calls=%fused_computation.6 | loop fusion | flops 7077888 | bytes 21233664 | tf_op jit(solution)/shard_map/convert_element_type | solution.py:268
  (198 shorter events, 154.9 us)
Async XLA Ops:
  7.2 311.5 %copy-start = (bf16[768,768]{1,0:T(8,128)(2,1)S(1)}, bf16[768,768]{1,0:T(8,128)(2,1)}, u32[]{:S(2)}) copy-start(bf16[768,768]{1,0:T(8,128)(2,1)} %param.35) | copy-start | bytes 3538948
  49.1 15.7 %copy-start.13 = (s32[8,128,128]{2,1,0:T(8,128)S(1)}, s32[8,128,128]{2,1,0:T(8,128)}, u32[]{:S(2)}) copy-start(s32[8,128,128]{2,1,0:T(8,128)} %param.21) | copy-start | bytes 1572868
  57.3 9.7 %copy-start.28 = (f32[12,32]{1,0:T(8,128)S(1)}, f32[12,32]{1,0:T(8,128)}, u32[]{:S(2)}) copy-start(f32[12,32]{1,0:T(8,128)} %param.29) | copy-start | bytes 4612
  60.6 38.8 %all-to-all-start = ((bf16[8,128,768]{2,1,0:T(8,128)(2,1)}), bf16[8,128,768]{2,1,0:T(8,128)(2,1)S(1)}, u32[]{:S(2)}, u32[]{:S(2)}) async-start(bf16[8,128,768]{2,1,0:T(8,128)(2,1)} %dynamic-slice_dynamic-update-slice_fusion.8), calls=%async_computation | async-start | bytes 3145728 | tf_op jit(solution)/shard_map/all_to_all | solution.py:204
  64.1 122.6 %all-gather.6.cloned.1.call-start = ((), (), s32[]{:S(2)}) async-start(), calls=%async_computation.3 | async-start | bytes 1769472 | tf_op jit(solution)/shard_map/all_gather | solution.py:213
  75.2 8.5 %copy-start.27 = (s32[8,128]{1,0:T(8,128)S(1)}, s32[8,128]{1,0:T(8,128)}, u32[]{:S(2)}) copy-start(s32[8,128]{1,0:T(8,128)} %param.22) | copy-start | bytes 12292
  75.2 8.7 %copy-start.31 = (f32[12]{0:T(128)S(1)}, f32[12]{0:T(128)}, u32[]{:S(2)}) copy-start(f32[12]{0:T(128)} %param.30) | copy-start | bytes 148
  94.3 18.0 %copy-start.30 = (s32[256]{0:T(256)S(1)}, s32[256]{0:T(256)}, u32[]{:S(2)}) copy-start(s32[256]{0:T(256)} %param.24) | copy-start | bytes 3076
  94.3 47.9 %copy-start.29 = (bf16[12,128]{1,0:T(8,128)(2,1)S(1)}, bf16[12,128]{1,0:T(8,128)(2,1)}, u32[]{:S(2)}) copy-start(bf16[12,128]{1,0:T(8,128)(2,1)} %param.28) | copy-start | bytes 9220
  94.3 77.4 %copy-start.5 = (bf16[4,128,768]{2,1,0:T(8,128)(2,1)S(1)}, bf16[4,128,768]{2,1,0:T(8,128)(2,1)}, u32[]{:S(2)}) copy-start(bf16[4,128,768]{2,1,0:T(8,128)(2,1)} %param.37) | copy-start | bytes 2359300
  99.3 208.3 %all-to-all-start.1 = ((bf16[8,12,128,128]{2,3,1,0:T(8,128)(2,1)}), bf16[8,12,128,128]{2,3,1,0:T(8,128)(2,1)}, u32[]{:S(2)}, u32[]{:S(2)}) async-start(bf16[8,12,128,128]{2,3,1,0:T(8,128)(2,1)} %dynamic-slice_dynamic-update-slice_fusion), calls=%async_computation.1 | async-start | bytes 6291456 | tf_op jit(solution)/shard_map/all_to_all | solution.py:205
  104.0 138.8 %all-gather.4.cloned.1.call-start = ((), (), s32[]{:S(2)}) async-start(), calls=%async_computation.2 | async-start | bytes 1769472 | tf_op jit(solution)/shard_map/all_gather | solution.py:214
  104.8 572.5 %all-reduce.3.cloned.1.call-start = ((), (), s32[]{:S(2)}) async-start(), calls=%async_computation.4 | async-start | bytes 28311552 | tf_op jit(solution)/shard_map/psum | solution.py:268
  307.6 2.7 copy-start.4
  342.8 46.4 %copy-start.6 = (bf16[4,128,768]{2,1,0:T(8,128)(2,1)S(1)}, bf16[4,128,768]{2,1,0:T(8,128)(2,1)}, u32[]{:S(2)}) copy-start(bf16[4,128,768]{2,1,0:T(8,128)(2,1)} %param.37) | copy-start | bytes 2359300
  389.1 3.0 copy-start.33
  401.6 6.9 copy-start.3
  408.5 6.7 copy-start.16
  408.5 6.7 copy-start.19
  408.5 6.7 copy-start.22
  408.5 6.7 copy-start.25
  415.2 3.5 copy-start.35
  423.3 4.5 copy-start.1
  423.3 4.5 copy-start.7
  (17 other events, 30.5 us)
Sparse Core Ops, SparseCore 0:
  66.8 27.1 all-gather.5
  106.8 27.0 all-gather.3
  430.2 247.0 all-reduce.2

commit v2 on v1

v2 whole, which is shorter than its diff:
```python
import math

import jax
import jax.numpy as jnp
from jax import lax
from jax.experimental import pallas as pl
from jax.experimental.pallas import tpu as pltpu
from jax.sharding import PartitionSpec as P

masked_value = -30000.0
half = 64
lanes = 128
extra_rows = 16
vmem_bytes = 60 * 1024 * 1024


def pick(array, index):
    rows = [lax.dynamic_slice_in_dim(array, index[i], 1, 0) for i in range(index.shape[0])]
    return jnp.concatenate(rows, axis=0)


def dot(left, right):
    return lax.dot_general(left, right, (((1,), (0,)), ((), ())), preferred_element_type=jnp.float32)


def dot_rows(left, right):
    return lax.dot_general(left, right, (((1,), (1,)), ((), ())), preferred_element_type=jnp.float32)


def dot_columns(left, right):
    return lax.dot_general(left, right, (((0,), (0,)), ((), ())), preferred_element_type=jnp.float32)


def narrow(values):
    return values.astype(jnp.bfloat16)


def pack_kernel(picked, atoms, bins, bonds, molecule, payload):
    rows, width = atoms.shape[1], atoms.shape[2]
    payload[0, :rows, :width] = atoms[0]
    payload[0, :rows, width : width + lanes] = narrow(bins[0].astype(jnp.float32))
    payload[0, :rows, width + lanes :] = narrow(bonds[0].astype(jnp.float32))
    payload[0, rows:, :] = jnp.zeros((extra_rows, width + 2 * lanes), jnp.bfloat16)
    molecule_rows = jnp.broadcast_to(molecule[0].astype(jnp.float32), (extra_rows, lanes))
    payload[0, rows:, :lanes] = narrow(molecule_rows)


def pack_blocks(picked, atoms, bins, bonds, molecule):
    _, rows, width = atoms.shape
    sent = picked.shape[0]

    def own(i, picked):
        return (picked[i], 0, 0)

    return pl.pallas_call(
        pack_kernel,
        grid_spec=pltpu.PrefetchScalarGridSpec(
            num_scalar_prefetch=1,
            grid=(sent,),
            in_specs=[
                pl.BlockSpec((1, rows, width), own),
                pl.BlockSpec((1, rows, rows), own),
                pl.BlockSpec((1, rows, rows), own),
                pl.BlockSpec((1, 1, rows), own),
            ],
            out_specs=pl.BlockSpec(
                (1, rows + extra_rows, width + 2 * lanes), lambda i, picked: (i, 0, 0)
            ),
        ),
        out_shape=jax.ShapeDtypeStruct((sent, rows + extra_rows, width + 2 * lanes), jnp.bfloat16),
        name="pack_blocks",
    )(picked, atoms, bins, bonds, molecule[:, None, :])


def both_halves(pair):
    lane = lax.broadcasted_iota(jnp.int32, (1, lanes), 1)
    first = narrow((lane < half).astype(jnp.float32))
    second = narrow((lane >= half).astype(jnp.float32))
    return jnp.concatenate([pair * first, pair * second], axis=0)


def side_by_side(stacked):
    rows = stacked.shape[0] // 2
    return jnp.concatenate([stacked[:rows], stacked[rows:]], axis=1)


def softmax_rows(scores):
    raised = jnp.exp(scores - jnp.max(scores, axis=-1, keepdims=True))
    return raised * (1.0 / jnp.sum(raised, axis=-1, keepdims=True))


def softmax_back(probs, d_probs, scale):
    inner = jnp.sum(probs * d_probs, axis=-1, keepdims=True)
    return narrow(probs * (d_probs - inner) * scale)


def layer_kernel(
    position, chosen, got, pocket, cross_bias, table, w_query, w_key, w_value, w_out, w_cquery,
    w_cout, cotangent, updated, grads, x, query, key, value, attended, middle, cquery, cattended,
    d_cross, d_cquery, d_middle, d_attended, d_query, d_key, d_value, code, probs
):
    rows = got.shape[1] - extra_rows
    width = x.shape[1]
    blocks = x.shape[0] // rows
    pairs = width // lanes
    per_block = chosen.shape[0] // blocks
    scale = 1.0 / math.sqrt(half)
    for b in range(blocks):
        block = got.at[position[b]]
        x[b * rows : (b + 1) * rows, :] = block[:rows, :width]
        bins = block[:rows, width : width + lanes].astype(jnp.float32)
        bonds = block[:rows, width + lanes :].astype(jnp.float32)
        molecule = block[rows:, :lanes].astype(jnp.float32)
        along = jnp.broadcast_to(molecule[0:1], (rows, lanes))
        live = bins + 32.0 * bonds
        code[b] = jnp.where(along == along.T, live, 64.0).astype(jnp.int32)
    query[...] = narrow(dot(x[...], w_query[...]))
    key[...] = narrow(dot(x[...], w_key[...]))
    value[...] = narrow(dot(x[...], w_value[...]))

    def place(step):
        b, p = step // pairs, step % pairs
        return b, p, pl.ds(pl.multiple_of(b * rows, rows), rows), pl.ds(pl.multiple_of(p * lanes, lanes), lanes)

    @pl.loop(0, blocks * pairs)
    def _(step):
        b, p, at, columns = place(step)
        index = code[b]
        bias = jnp.concatenate(
            [
                jnp.take_along_axis(
                    jnp.broadcast_to(table[2 * p + h], (rows, lanes)), index, axis=1, mode="promise_in_bounds"
                )
                for h in range(2)
            ],
            axis=0,
        )
        scores = dot_rows(both_halves(query[at, columns]), key[at, columns]) * scale + bias
        weights = softmax_rows(scores)
        probs[step] = weights
        rounded = side_by_side(narrow(weights))
        attended[at, columns] = narrow(dot(rounded, both_halves(value[at, columns])))

    middle[...] = narrow(x[...].astype(jnp.float32) + dot(attended[...], w_out[...]))
    cquery[...] = narrow(dot(middle[...], w_cquery[...]))
    d_cross[...] = narrow(dot_rows(cotangent[...], w_cout[...]))

    @pl.loop(0, blocks * pairs)
    def _(step):
        b, p, at, columns = place(step)
        far = pl.ds(pl.multiple_of(width + p * lanes, lanes), lanes)
        picks = [chosen[b * per_block + t] for t in range(per_block)]
        keys = jnp.concatenate([pocket[c, :rows, columns] for c in picks], axis=0)
        values = jnp.concatenate([pocket[c, :rows, far] for c in picks], axis=0)
        bias = jnp.concatenate(
            [
                jnp.broadcast_to(
                    jnp.concatenate([cross_bias[c, 2 * p + h] for c in picks], axis=1),
                    (rows, per_block * rows),
                )
                for h in range(2)
            ],
            axis=0,
        )
        weights = softmax_rows(dot_rows(both_halves(cquery[at, columns]), keys) * scale + bias)
        rounded = side_by_side(narrow(weights))
        cattended[at, columns] = narrow(dot(rounded, both_halves(values)))
        d_weights = dot_rows(both_halves(d_cross[at, columns]), values)
        d_scores = side_by_side(softmax_back(weights, d_weights, scale))
        d_cquery[at, columns] = narrow(dot(d_scores, both_halves(keys)))

    updated[...] = narrow(middle[...].astype(jnp.float32) + dot(cattended[...], w_cout[...]))
    d_middle[...] = narrow(cotangent[...].astype(jnp.float32) + dot_rows(d_cquery[...], w_cquery[...]))
    d_attended[...] = narrow(dot_rows(d_middle[...], w_out[...]))
    grads[5] = dot_columns(cattended[...], cotangent[...]).astype(grads.dtype)
    grads[4] = dot_columns(middle[...], d_cquery[...]).astype(grads.dtype)
    grads[3] = dot_columns(attended[...], d_middle[...]).astype(grads.dtype)

    @pl.loop(0, blocks * pairs)
    def _(step):
        b, p, at, columns = place(step)
        weights = probs[step]
        d_att = both_halves(d_attended[at, columns])
        d_weights = dot_rows(d_att, value[at, columns])
        d_scores = softmax_back(weights, d_weights, scale)
        d_query[at, columns] = narrow(dot(side_by_side(d_scores), both_halves(key[at, columns])))
        d_key[at, columns] = narrow(dot_columns(d_scores, both_halves(query[at, columns])))
        d_value[at, columns] = narrow(dot_columns(narrow(weights), d_att))

    grads[0] = dot_columns(x[...], d_query[...]).astype(grads.dtype)
    grads[1] = dot_columns(x[...], d_key[...]).astype(grads.dtype)
    grads[2] = dot_columns(x[...], d_value[...]).astype(grads.dtype)


def layer(position, chosen, got, pocket, cross_bias, table, weights, cotangent):
    total_rows, width = cotangent.shape
    rows = got.shape[1] - extra_rows
    blocks = total_rows // rows
    pairs = width // lanes
    whole = pl.BlockSpec(memory_space=pltpu.VMEM)
    scalar = pl.BlockSpec(memory_space=pltpu.SMEM)
    return pl.pallas_call(
        layer_kernel,
        in_specs=[scalar, scalar] + [whole] * 11,
        out_specs=[whole, whole],
        out_shape=[
            jax.ShapeDtypeStruct((total_rows, width), jnp.bfloat16),
            jax.ShapeDtypeStruct((6, width, width), jnp.bfloat16),
        ],
        scratch_shapes=[pltpu.VMEM((total_rows, width), jnp.bfloat16)] * 15
        + [
            pltpu.VMEM((blocks, rows, lanes), jnp.int32),
            pltpu.VMEM((blocks * pairs, 2 * rows, rows), jnp.float32),
        ],
        compiler_params=pltpu.CompilerParams(vmem_limit_bytes=vmem_bytes),
        name="layer",
    )(position, chosen, got, pocket, cross_bias, table, *weights, cotangent)


def on_device(
    atoms,
    distance_bins,
    bonds,
    molecule,
    block_counts,
    block_scaffold,
    pocket_ids,
    pocket_keys,
    pocket_values,
    pocket_bias,
    bin_table,
    bond_weight,
    w_query,
    w_key,
    w_value,
    w_out,
    w_cross_query,
    w_cross_out,
    cotangent,
):
    dp_count = lax.axis_size("dp")
    pocket_count = lax.axis_size("pocket")
    capacity = atoms.shape[0]
    balanced = cotangent.shape[0]
    row_count = atoms.shape[1]
    width = atoms.shape[2]
    heads = bin_table.shape[0]
    bin_count = bin_table.shape[1]
    per_target = -(-capacity // dp_count)
    pocket_rows = jnp.concatenate(
        [
            jnp.concatenate([pocket_keys, pocket_values], axis=1),
            jnp.pad(pocket_bias, ((0, extra_rows - heads), (0, 2 * width - pocket_bias.shape[1]))),
        ],
        axis=0,
    )
    pocket = lax.all_gather(pocket_rows, "pocket", axis=0)
    cross_bias = pocket[:, row_count : row_count + heads, None, :row_count].astype(jnp.float32)
    counts = lax.all_gather(block_counts.reshape(1), "dp", axis=0, tiled=True)
    places = lax.broadcasted_iota(jnp.int32, (dp_count, dp_count), 0)
    before = places > lax.broadcasted_iota(jnp.int32, (dp_count, dp_count), 1)
    offsets = jnp.sum(jnp.where(before, counts[None, :], 0), axis=1)
    own_device = lax.axis_index("dp")
    own_column = lax.axis_index("pocket")
    own_offset = offsets[own_device]
    own_count = counts[own_device]
    target_rows = lax.broadcasted_iota(jnp.int32, (dp_count, per_target), 0)
    turn_index = lax.broadcasted_iota(jnp.int32, (dp_count, per_target), 1)
    outgoing = jnp.mod(target_rows - own_offset, dp_count) + dp_count * turn_index
    picked = jnp.where(outgoing < own_count, outgoing, 0).reshape(-1)
    source_offset = offsets[:, None]
    source_count = counts[:, None]
    incoming = jnp.mod(own_device - source_offset, dp_count) + dp_count * turn_index
    usable = incoming < source_count
    landing = (source_offset + incoming) // dp_count
    wanted = lax.broadcasted_iota(jnp.int32, (balanced, 1), 0)
    matches = (landing.reshape(1, -1) == wanted) & usable.reshape(1, -1)
    received_index = lax.broadcasted_iota(jnp.int32, (balanced, dp_count * per_target), 1)
    position = jnp.sum(jnp.where(matches, received_index, 0), axis=1)
    anchors = ((target_rows * pocket_count + own_column) * capacity + incoming).reshape(1, -1)
    anchor = jnp.sum(jnp.where(matches, anchors, 0), axis=1)
    payload = pack_blocks(picked, atoms, distance_bins, bonds, molecule)
    got = lax.all_to_all(payload, "dp", split_axis=0, concat_axis=0, tiled=True)
    scaffold = pick(block_scaffold, anchor)
    ids = pocket_ids.T
    chosen = jnp.concatenate(
        [lax.dynamic_slice_in_dim(ids, scaffold[b], 1, 1)[:, 0] for b in range(balanced)]
    )
    table = jnp.concatenate(
        [
            bin_table,
            bin_table + bond_weight[:, None],
            jnp.full((heads, lanes - 2 * bin_count), masked_value, jnp.float32),
        ],
        axis=1,
    )
    table = lax.reduce_precision(table, 8, 7)[:, None, :]
    weights = (w_query, w_key, w_value, w_out, w_cross_query, w_cross_out)
    updated, grads = layer(
        position, chosen, got, pocket, cross_bias, table, weights, cotangent.reshape(-1, width)
    )
    scale = 1.0 / math.sqrt(balanced * row_count * dp_count * pocket_count)
    rows = grads.reshape(6 * width, width)
    share = lax.psum_scatter(rows, ("dp", "pocket"), scatter_dimension=0, tiled=True)
    share = (share.astype(jnp.float32) * scale).astype(jnp.bfloat16)
    weight_grads = lax.all_gather(share, ("dp", "pocket"), axis=0, tiled=True)
    return (updated.reshape(cotangent.shape), weight_grads.reshape(6, width, width))


def solution(mesh):
    return jax.shard_map(
        on_device,
        mesh=mesh,
        in_specs=(
            P(("dp", "pocket"), None, None),
            P(("dp", "pocket"), None, None),
            P(("dp", "pocket"), None, None),
            P(("dp", "pocket"), None),
            P("dp", "pocket"),
            P(),
            P(),
            P("pocket", None),
            P("pocket", None),
            P(None, "pocket"),
            P(),
            P(),
            P(),
            P(),
            P(),
            P(),
            P(),
            P(),
            P(("dp", "pocket"), None, None),
        ),
        out_specs=(P(("dp", "pocket"), None, None), P()),
        check_vma=False,
    )
```

time: 706 us -> 361 us (0.51); the launches traced: 693 us -> 360 us
  local copies, waits for them, and re-layouts: 170 us -> 14.2 us
  matrix products: 137 us -> 0 us
  Pallas kernels: 0 us -> 69 us
  between operations: 82.9 us -> 28.3 us
  waiting for transfers between devices: 251 us -> 225 us
  other arithmetic: 25 us -> 9.63 us
  blocking collectives: 19 us -> 9.92 us
    psum x1 -> x0, waiting for transfers between devices: 244 us -> none  [on_device(): lax.psum(total, ('dp', 'pocket')) * scale]
    dot_general x25 -> x0, matrix products: 132 us -> none  [the longest x9 89.9 us: einsum_mixed(): return jnp.einsum(form, left, right, preferred_element_type=jnp.float32)]
    reduce_scatter x0 -> x1, waiting for transfers between devices: none -> 119 us  [on_device(): lax.psum_scatter(rows, ('dp', 'pocket'), scatter_dimension=0, tiled=True)]
    all_gather x2, waiting for transfers between devices: 0.01 us -> 74 us  [the longest x1 74 us: on_device(): weight_grads = lax.all_gather(share, ('dp', 'pocket'), axis=0, tiled=True)]
    unnamed x123 -> x13, local copies, waits for them, and re-layouts: 79.4 us -> 10.4 us
    pallas_call x0 -> x2, Pallas kernels: none -> 69 us  [the longest x1 63.4 us: layer(): pl.pallas_call(layer_kernel, in_specs=[scalar, scalar] + [whole] * 11, ou...]
    concatenate x6 -> x3, local copies, waits for them, and re-layouts: 41.5 us -> 0.09 us  [on_device(): jnp.concatenate([bin_table, bin_table + bond_weight[:, None], jnp.full((h...]
    all_to_all x2 -> x1, waiting for transfers between devices: 4.99 us -> 31.5 us  [on_device(): got = lax.all_to_all(payload, 'dp', split_axis=0, concat_axis=0, tiled=True)]
  transfers between devices with their start and end apart: 5 -> 4, of which waited for: 2 -> 3; matrix products, arithmetic and copies ran while one was open for 26% -> 3% of each run, Pallas kernels for 0% -> 2%
where the time goes in v2:
time: 361 us; the launch traced here: 360 us
  waiting for transfers between devices  225 us (62%)
  Pallas kernels  69 us (19%)
  between operations  28.3 us (8%)
  local copies, waits for them, and re-layouts  14.2 us (4%)
  blocking collectives  9.92 us (3%)
  other arithmetic  9.63 us (3%)
  starting transfers between devices  4 us (1%)
    reduce_scatter x1, waiting for transfers between devices, on_device(): lax.psum_scatter(rows, ('dp', 'pocket'), scatter_dimension=0, tiled=True)  119 us
    all_gather x1, waiting for transfers between devices, on_device(): weight_grads = lax.all_gather(share, ('dp', 'pocket'), axis=0, tiled=True)  74 us
    pallas_call x1, Pallas kernels, layer(): pl.pallas_call(layer_kernel, in_specs=[scalar, scalar] + [whole] * 11, ou...  63.4 us
    all_to_all x1, waiting for transfers between devices, on_device(): got = lax.all_to_all(payload, 'dp', split_axis=0, concat_axis=0, tiled=True)  31.5 us
    unnamed x13, local copies, waits for them, and re-layouts  10.4 us
    all_gather x1, blocking collectives, on_device(): counts = lax.all_gather(block_counts.reshape(1), 'dp', axis=0, tiled=True)  9.92 us
  transfers between devices with their start and end apart: 4, of which 3 were waited for; matrix products, arithmetic and copies ran while one was open for 3% of the time, Pallas kernels for 2%

profile of v2, /device:TPU:0, one launch (start us, length us, event | category | flops | bytes accessed | tf_op | source)
XLA Modules:
  0.0 359.8 jit_solution(12191447443189958859)
XLA Ops:
  7.2 1.8 fusion.1
  9.7 1.2 dynamic-slice.17
  11.0 0.7 bitcast_dynamic-update-slice_fusion
  11.6 9.9 %all-reduce.1 = s32[4]{0:T(128)S(1)} all-reduce(s32[4]{0:T(128)S(1)} %bitcast_dynamic-update-slice_fusion), channel_id=2, replica_groups=mesh['dp'=4,'pocket'=8] {'dp'}, use_global_device_ids=true, to_apply=%add.1 | all-reduce | flops 4 | bytes 32 | tf_op jit(solution)/shard_map/all_gather | solution.py:259
  22.9 0.7 compare_and_fusion
  23.5 0.7 broadcast_add_fusion.1
  24.2 0.7 compare_select_fusion.1
  25.1 1.1 compare_select_fusion
  26.2 5.6 %pack_blocks.1 = bf16[8,144,1024]{2,1,0:T(8,128)(2,1)} custom-call(s32[8]{0:T(128)} %get-tuple-element.23.picked, bf16[8,128,768]{2,1,0:T(8,128)(2,1)} %atoms.1, s32[8,128,128]{2,1,0:T(8,128)} %bins.1, s32[8,128,128]{2,1,0:T(8,128)} %bonds.1, s32[8,1,128]{2,1,0:T(1,128)} %bitcast.29), custom_call_target="tpu_custom_call" | custom-call | tf_op jit(solution)/shard_map/pack_blocks/pallas_call | solution.py:55
  31.8 3.9 %all-to-all-start = ((bf16[8,144,1024]{2,1,0:T(8,128)(2,1)}), bf16[8,144,1024]{2,1,0:T(8,128)(2,1)S(1)}, u32[]{:S(2)}, u32[]{:S(2)}) async-start(bf16[8,144,1024]{2,1,0:T(8,128)(2,1)} %pack_blocks.1), calls=%async_computation | async-start | bytes 4718592 | tf_op jit(solution)/shard_map/all_to_all | solution.py:283
  36.0 0.7 select_reduce_fusion
  44.2 0.6 fusion.6
  51.9 1.0 dynamic-slice_reduce_fusion.3
  52.9 0.6 pad_add_fusion.chosen
  53.5 0.7 maximum_reduce-precision_fusion.table
  54.2 0.8 fusion.2
  54.9 0.7 copy.26.cross_bias
  55.6 31.5 %all-to-all-done.got = bf16[8,144,1024]{2,1,0:T(8,128)(2,1)S(1)} async-done(((bf16[8,144,1024]{2,1,0:T(8,128)(2,1)}), bf16[8,144,1024]{2,1,0:T(8,128)(2,1)S(1)}, u32[]{:S(2)}, u32[]{:S(2)}) %all-to-all-start) | async-done | bytes 2359328 | tf_op jit(solution)/shard_map/all_to_all | solution.py:283
  87.1 1.4 copy-done
  88.5 63.4 %layer.1 = (bf16[512,768]{1,0:T(8,128)(2,1)}, bf16[6,768,768]{2,1,0:T(8,128)(2,1)}) custom-call(s32[4]{0:T(128)} %get-tuple-element.11.position, s32[16]{0:T(128)} %pad_add_fusion.chosen, bf16[8,144,1024]{2,1,0:T(8,128)(2,1)} %copy-done, bf16[8,144,1536]{2,1,0:T(8,128)(2,1)} %bitcast.27, f32[8,12,1,128]{3,2,1,0:T(1,128)} %copy.26.cross_bias, ...), custom_call_target="tpu_custom_call" | custom-call | tf_op jit(solution)/shard_map/layer/pallas_call | solution.py:202
  152.0 119.2 %reduce-scatter.2.cloned.1.call-done = bf16[144,768]{1,0:T(8,128)(2,1)} async-done(((bf16[4608,768]{1,0:T(8,128)(2,1)}), bf16[144,768]{1,0:T(8,128)(2,1)}) %reduce-scatter.2.cloned.1.call-update) | async-done | bytes 221200 | tf_op jit(solution)/shard_map/reduce_scatter | solution.py:304
  271.2 1.7 multiply_convert_fusion
  272.9 74.0 %all-gather.5.cloned.1.call-done = bf16[4608,768]{1,0:T(8,128)(2,1)} async-done(((bf16[144,768]{1,0:T(8,128)(2,1)}), bf16[4608,768]{1,0:T(8,128)(2,1)}) %all-gather.5.cloned.1.call-update) | async-done | bytes 7077904 | tf_op jit(solution)/shard_map/all_gather | solution.py:306
  346.9 6.4 %copy.32 = bf16[6,768,768]{2,1,0:T(8,128)(2,1)} copy(bf16[6,768,768]{2,1,0:T(8,128)(2,1)} %bitcast.25) | data formatting | bytes 14155776
  (33 shorter events, 2.7 us)
Async XLA Ops:
  7.2 47.0 %all-gather.7.cloned.1.call-start = ((), (), s32[]{:S(2)}) async-start(), calls=%async_computation.4 | async-start | bytes 3981312 | tf_op jit(solution)/shard_map/all_gather | solution.py:257
  31.8 12.4 %copy-start.2 = (s32[256]{0:T(256)S(1)}, s32[256]{0:T(256)}, u32[]{:S(2)}) copy-start(s32[256]{0:T(256)} %param.24) | copy-start | bytes 3076
  31.8 17.6 %copy-start.1 = (f32[12,32]{1,0:T(8,128)S(1)}, f32[12,32]{1,0:T(8,128)}, u32[]{:S(2)}) copy-start(f32[12,32]{1,0:T(8,128)} %param.29) | copy-start | bytes 4612
  31.8 17.6 %copy-start.3 = (f32[12]{0:T(128)S(1)}, f32[12]{0:T(128)}, u32[]{:S(2)}) copy-start(f32[12]{0:T(128)} %param.30) | copy-start | bytes 148
  31.8 55.3 %all-to-all-start = ((bf16[8,144,1024]{2,1,0:T(8,128)(2,1)}), bf16[8,144,1024]{2,1,0:T(8,128)(2,1)S(1)}, u32[]{:S(2)}, u32[]{:S(2)}) async-start(bf16[8,144,1024]{2,1,0:T(8,128)(2,1)} %pack_blocks.1), calls=%async_computation | async-start | bytes 4718592 | tf_op jit(solution)/shard_map/all_to_all | solution.py:283
  35.7 235.5 %reduce-scatter.2.cloned.1.call-start = ((), (), s32[]{:S(2)}) async-start(), calls=%async_computation.2 | async-start | bytes 7299072 | tf_op jit(solution)/shard_map/reduce_scatter | solution.py:304
  87.1 1.4 copy-start
  151.9 194.9 %all-gather.5.cloned.1.call-start = ((), (), s32[]{:S(2)}) async-start(), calls=%async_computation.3 | async-start | bytes 7299072 | tf_op jit(solution)/shard_map/all_gather | solution.py:306
Sparse Core Ops, SparseCore 0:
  10.5 36.6 all-gather.6
  152.1 119.1 reduce-scatter.1
  275.1 71.7 all-gather.4

commit v3 on v2

--- a/solution.py
+++ b/solution.py
@@ -96,8 +96,8 @@
 
 def layer_kernel(
     position, chosen, got, pocket, cross_bias, table, w_query, w_key, w_value, w_out, w_cquery,
-    w_cout, cotangent, updated, grads, x, query, key, value, attended, middle, cquery, cattended,
-    d_cross, d_cquery, d_middle, d_attended, d_query, d_key, d_value, code, probs
+    w_cout, cotangent, updated, grads, x, query, key, value, d_attended, probs, attended, middle,
+    cquery, cattended, d_cross, d_cquery, d_middle, code
 ):
     rows = got.shape[1] - extra_rows
     width = x.shape[1]
@@ -172,13 +172,21 @@
     updated[...] = narrow(middle[...].astype(jnp.float32) + dot(cattended[...], w_cout[...]))
     d_middle[...] = narrow(cotangent[...].astype(jnp.float32) + dot_rows(d_cquery[...], w_cquery[...]))
     d_attended[...] = narrow(dot_rows(d_middle[...], w_out[...]))
-    grads[5] = dot_columns(cattended[...], cotangent[...]).astype(grads.dtype)
-    grads[4] = dot_columns(middle[...], d_cquery[...]).astype(grads.dtype)
-    grads[3] = dot_columns(attended[...], d_middle[...]).astype(grads.dtype)
-
-    @pl.loop(0, blocks * pairs)
+    grads[2] = dot_columns(cattended[...], cotangent[...]).astype(grads.dtype)
+    grads[1] = dot_columns(middle[...], d_cquery[...]).astype(grads.dtype)
+    grads[0] = dot_columns(attended[...], d_middle[...]).astype(grads.dtype)
+
+
+def self_back_kernel(x, query, key, value, d_attended, probs, grads, d_query, d_key, d_value):
+    steps, rows = probs.shape[0], probs.shape[2]
+    pairs = x.shape[1] // lanes
+    scale = 1.0 / math.sqrt(half)
+
+    @pl.loop(0, steps)
     def _(step):
-        b, p, at, columns = place(step)
+        b, p = step // pairs, step % pairs
+        at = pl.ds(pl.multiple_of(b * rows, rows), rows)
+        columns = pl.ds(pl.multiple_of(p * lanes, lanes), lanes)
         weights = probs[step]
         d_att = both_halves(d_attended[at, columns])
         d_weights = dot_rows(d_att, value[at, columns])
@@ -199,22 +207,34 @@
     pairs = width // lanes
     whole = pl.BlockSpec(memory_space=pltpu.VMEM)
     scalar = pl.BlockSpec(memory_space=pltpu.SMEM)
-    return pl.pallas_call(
+    flat = jax.ShapeDtypeStruct((total_rows, width), jnp.bfloat16)
+    half_grads = jax.ShapeDtypeStruct((3, width, width), jnp.bfloat16)
+    params = pltpu.CompilerParams(vmem_limit_bytes=vmem_bytes)
+    flat_scratch = pltpu.VMEM((total_rows, width), jnp.bfloat16)
+    updated, late_grads, *kept = pl.pallas_call(
         layer_kernel,
         in_specs=[scalar, scalar] + [whole] * 11,
-        out_specs=[whole, whole],
-        out_shape=[
-            jax.ShapeDtypeStruct((total_rows, width), jnp.bfloat16),
-            jax.ShapeDtypeStruct((6, width, width), jnp.bfloat16),
-        ],
-        scratch_shapes=[pltpu.VMEM((total_rows, width), jnp.bfloat16)] * 15
-        + [
-            pltpu.VMEM((blocks, rows, lanes), jnp.int32),
-            pltpu.VMEM((blocks * pairs, 2 * rows, rows), jnp.float32),
-        ],
-        compiler_params=pltpu.CompilerParams(vmem_limit_bytes=vmem_bytes),
+        out_specs=[whole] * 8,
+        out_shape=[flat, half_grads]
+        + [flat] * 5
+        + [jax.ShapeDtypeStruct((blocks * pairs, 2 * rows, rows), jnp.float32)],
+        scratch_shapes=[flat_scratch] * 7 + [pltpu.VMEM((blocks, rows, lanes), jnp.int32)],
+        compiler_params=params,
         name="layer",
     )(position, chosen, got, pocket, cross_bias, table, *weights, cotangent)
+    early_grads = pl.pallas_call(
+        self_back_kernel,
+        in_specs=[whole] * 6,
+        out_specs=whole,
+        out_shape=half_grads,
+        scratch_shapes=[flat_scratch] * 3,
+        compiler_params=params,
+        cost_estimate=pl.CostEstimate(
+            flops=12 * total_rows * width * width, bytes_accessed=12 * total_rows * width * 2, transcendentals=0
+        ),
+        name="self_back",
+    )(*kept)
+    return updated, early_grads, late_grads
 
 
 def on_device(
@@ -296,15 +316,22 @@
     )
     table = lax.reduce_precision(table, 8, 7)[:, None, :]
     weights = (w_query, w_key, w_value, w_out, w_cross_query, w_cross_out)
-    updated, grads = layer(
+    updated, early_grads, late_grads = layer(
         position, chosen, got, pocket, cross_bias, table, weights, cotangent.reshape(-1, width)
     )
     scale = 1.0 / math.sqrt(balanced * row_count * dp_count * pocket_count)
-    rows = grads.reshape(6 * width, width)
-    share = lax.psum_scatter(rows, ("dp", "pocket"), scatter_dimension=0, tiled=True)
-    share = (share.astype(jnp.float32) * scale).astype(jnp.bfloat16)
-    weight_grads = lax.all_gather(share, ("dp", "pocket"), axis=0, tiled=True)
-    return (updated.reshape(cotangent.shape), weight_grads.reshape(6, width, width))
+
+    def summed(grads):
+        share = lax.psum_scatter(
+            grads.reshape(-1, width), ("dp", "pocket"), scatter_dimension=0, tiled=True
+        )
+        share = (share.astype(jnp.float32) * scale).astype(jnp.bfloat16)
+        return lax.all_gather(share, ("dp", "pocket"), axis=0, tiled=True).reshape(grads.shape)
+
+    late = summed(late_grads)
+    early = summed(early_grads)
+    weight_grads = jnp.concatenate([early, late], axis=0)
+    return (updated.reshape(cotangent.shape), weight_grads)
 
 
 def solution(mesh):

time: 361 us -> 486 us (1.35)
  waiting for transfers between devices: 225 us -> 345 us
  other arithmetic: 9.63 us -> 17.7 us
  local copies, waits for them, and re-layouts: 14.2 us -> 7.82 us
    reduce_scatter x1 -> x2, waiting for transfers between devices: 119 us -> 191 us  [summed(): lax.psum_scatter(grads.reshape(-1, width), ('dp', 'pocket'), scatter_dime...]
    all_gather x1 -> x2, waiting for transfers between devices: 74 us -> 122 us  [summed(): lax.all_gather(share, ('dp', 'pocket'), axis=0, tiled=True)]
    pallas_call x0 -> x1, Pallas kernels: none -> 18.3 us  [layer(): pl.pallas_call(self_back_kernel, in_specs=[whole] * 6, out_specs=whole, o...]
    pallas_call x1, Pallas kernels: 63.4 us -> 49 us  [layer(): pl.pallas_call(layer_kernel, in_specs=[scalar, scalar] + [whole] * 11, ou...]
    concatenate x0 -> x1, other arithmetic: none -> 6.65 us  [on_device(): weight_grads = jnp.concatenate([early, late], axis=0)]
    unnamed x13 -> x12, local copies, waits for them, and re-layouts: 10.4 us -> 3.99 us
  transfers between devices with their start and end apart: 4 -> 6, of which waited for: 3 -> 5; matrix products, arithmetic and copies ran while one was open for 3% -> 3% of each run, Pallas kernels for 2% -> 5%
where the time goes in v3:
time: 486 us
  waiting for transfers between devices  345 us (71%)
  Pallas kernels  72.9 us (15%)
  between operations  28.4 us (6%)
  other arithmetic  17.7 us (4%)
  blocking collectives  9.92 us (2%)
  local copies, waits for them, and re-layouts  7.82 us (2%)
    reduce_scatter x2, waiting for transfers between devices, summed(): lax.psum_scatter(grads.reshape(-1, width), ('dp', 'pocket'), scatter_dime...  191 us
    all_gather x2, waiting for transfers between devices, summed(): lax.all_gather(share, ('dp', 'pocket'), axis=0, tiled=True)  122 us
    pallas_call x1, Pallas kernels, layer(): pl.pallas_call(layer_kernel, in_specs=[scalar, scalar] + [whole] * 11, ou...  49 us
    all_to_all x1, waiting for transfers between devices, on_device(): got = lax.all_to_all(payload, 'dp', split_axis=0, concat_axis=0, tiled=True)  32.1 us
    pallas_call x1, Pallas kernels, layer(): pl.pallas_call(self_back_kernel, in_specs=[whole] * 6, out_specs=whole, o...  18.3 us
    all_gather x1, blocking collectives, on_device(): counts = lax.all_gather(block_counts.reshape(1), 'dp', axis=0, tiled=True)  9.92 us
  transfers between devices with their start and end apart: 6, of which 5 were waited for; matrix products, arithmetic and copies ran while one was open for 3% of the time, Pallas kernels for 5%

profile of v3, /device:TPU:0, one launch (start us, length us, event | category | flops | bytes accessed | tf_op | source)
XLA Modules:
  0.0 485.9 jit_solution(6678328429734663354)
XLA Ops:
  7.2 1.8 fusion.1
  9.7 1.2 dynamic-slice.17
  11.0 0.7 bitcast_dynamic-update-slice_fusion
  11.6 9.9 %all-reduce.1 = s32[4]{0:T(128)S(1)} all-reduce(s32[4]{0:T(128)S(1)} %bitcast_dynamic-update-slice_fusion), channel_id=2, replica_groups=mesh['dp'=4,'pocket'=8] {'dp'}, use_global_device_ids=true, to_apply=%add.1 | all-reduce | flops 4 | bytes 32 | tf_op jit(solution)/shard_map/all_gather | solution.py:279
  23.5 0.7 broadcast_add_fusion.1
  25.1 1.1 compare_select_fusion
  26.2 5.6 %pack_blocks.1 = bf16[8,144,1024]{2,1,0:T(8,128)(2,1)} custom-call(s32[8]{0:T(128)} %get-tuple-element.35.picked, bf16[8,128,768]{2,1,0:T(8,128)(2,1)} %atoms.1, s32[8,128,128]{2,1,0:T(8,128)} %bins.1, s32[8,128,128]{2,1,0:T(8,128)} %bonds.1, s32[8,1,128]{2,1,0:T(1,128)} %bitcast.33), custom_call_target="tpu_custom_call" | custom-call | tf_op jit(solution)/shard_map/pack_blocks/pallas_call | solution.py:55
  31.8 3.8 all-to-all-start
  51.8 1.0 dynamic-slice_reduce_fusion.3
  52.7 0.7 pad_add_fusion.chosen
  53.4 0.7 maximum_reduce-precision_fusion.table
  54.1 0.8 fusion.2
  54.8 0.7 copy.26.cross_bias
  55.5 32.1 %all-to-all-done.got = bf16[8,144,1024]{2,1,0:T(8,128)(2,1)S(1)} async-done(((bf16[8,144,1024]{2,1,0:T(8,128)(2,1)}), bf16[8,144,1024]{2,1,0:T(8,128)(2,1)S(1)}, u32[]{:S(2)}, u32[]{:S(2)}) %all-to-all-start) | async-done | bytes 2359328 | tf_op jit(solution)/shard_map/all_to_all | solution.py:303
  87.6 1.5 copy-done
  89.1 49.0 %layer.1 = (bf16[512,768]{1,0:T(8,128)(2,1)}, bf16[3,768,768]{2,1,0:T(8,128)(2,1)}, bf16[512,768]{1,0:T(8,128)(2,1)}, bf16[512,768]{1,0:T(8,128)(2,1)}, bf16[512...) custom-call(s32[4]{0:T(128)} %get-tuple-element.23.position, ...), custom_call_target="tpu_custom_call" | custom-call | tf_op jit(solution)/shard_map/layer/pallas_call | solution.py:214
  138.2 18.3 %self_back.1 = bf16[3,768,768]{2,1,0:T(8,128)(2,1)} custom-call(bf16[512,768]{1,0:T(8,128)(2,1)} %get-tuple-element.11.x, bf16[512,768]{1,0:T(8,128)(2,1)} %get-tuple-element.12.query, bf16[512,768]{1,0:T(8,128)(2,1)} %get-tuple-element.13.key, bf16[512,768]{1,0:T(8,128)(2,1)} %get-tuple-element.14.value, bf16[512,768]{1,0:T(8,128)(2,1)} %get-tuple-element.15.d_attended, ...), custom_call_target="tpu_custom_call" | custom-call | flops 3623878656 | bytes 9437184 | tf_op jit(solution)/shard_map/self_back/pallas_call | solution.py:225
  156.5 84.8 %reduce-scatter.5.cloned.1.call-done = bf16[72,768]{1,0:T(8,128)(2,1)} async-done(((bf16[2304,768]{1,0:T(8,128)(2,1)}), bf16[72,768]{1,0:T(8,128)(2,1)}) %reduce-scatter.5.cloned.1.call-update) | async-done | bytes 110608 | tf_op jit(solution)/shard_map/reduce_scatter | solution.py:325
  241.3 1.6 multiply_convert_fusion
  242.9 105.8 %reduce-scatter.3.cloned.1.call-done = bf16[72,768]{1,0:T(8,128)(2,1)} async-done(((bf16[2304,768]{1,0:T(8,128)(2,1)}), bf16[72,768]{1,0:T(8,128)(2,1)}) %reduce-scatter.3.cloned.1.call-update) | async-done | bytes 110608 | tf_op jit(solution)/shard_map/reduce_scatter | solution.py:325
  348.7 1.6 multiply_convert_fusion.1
  350.3 60.8 %all-gather.8.cloned.1.call-done = bf16[2304,768]{1,0:T(8,128)(2,1)} async-done(((bf16[72,768]{1,0:T(8,128)(2,1)}), bf16[2304,768]{1,0:T(8,128)(2,1)}) %all-gather.8.cloned.1.call-update) | async-done | bytes 3538960 | tf_op jit(solution)/shard_map/all_gather | solution.py:329
  411.1 61.6 %all-gather.6.cloned.1.call-done = bf16[2304,768]{1,0:T(8,128)(2,1)} async-done(((bf16[72,768]{1,0:T(8,128)(2,1)}), bf16[2304,768]{1,0:T(8,128)(2,1)}) %all-gather.6.cloned.1.call-update) | async-done | bytes 3538960 | tf_op jit(solution)/shard_map/all_gather | solution.py:329
  472.7 6.6 %pad_maximum_fusion = bf16[6,768,768]{2,1,0:T(8,128)(2,1)} fusion(bf16[3,768,768]{2,1,0:T(8,128)(2,1)} %bitcast.28, bf16[3,768,768]{2,1,0:T(8,128)(2,1)} %bitcast.29), kind=kLoop, calls=%fused_computation | loop fusion | flops 3538944 | bytes 14155776 | tf_op jit(solution)/shard_map/concatenate | solution.py:333
  (41 shorter events, 5.4 us)
Async XLA Ops:
  7.2 46.9 %all-gather.10.cloned.1.call-start = ((), (), s32[]{:S(2)}) async-start(), calls=%async_computation.7 | async-start | bytes 3981312 | tf_op jit(solution)/shard_map/all_gather | solution.py:277
  31.8 12.2 %copy-start.2 = (s32[256]{0:T(256)S(1)}, s32[256]{0:T(256)}, u32[]{:S(2)}) copy-start(s32[256]{0:T(256)} %param.24) | copy-start | bytes 3076
  31.8 17.5 %copy-start.1 = (f32[12,32]{1,0:T(8,128)S(1)}, f32[12,32]{1,0:T(8,128)}, u32[]{:S(2)}) copy-start(f32[12,32]{1,0:T(8,128)} %param.29) | copy-start | bytes 4612
  31.8 17.5 %copy-start.3 = (f32[12]{0:T(128)S(1)}, f32[12]{0:T(128)}, u32[]{:S(2)}) copy-start(f32[12]{0:T(128)} %param.30) | copy-start | bytes 148
  31.8 55.8 %all-to-all-start = ((bf16[8,144,1024]{2,1,0:T(8,128)(2,1)}), bf16[8,144,1024]{2,1,0:T(8,128)(2,1)S(1)}, u32[]{:S(2)}, u32[]{:S(2)}) async-start(bf16[8,144,1024]{2,1,0:T(8,128)(2,1)} %pack_blocks.1), calls=%async_computation | async-start | bytes 4718592 | tf_op jit(solution)/shard_map/all_to_all | solution.py:303
  35.6 205.7 %reduce-scatter.5.cloned.1.call-start = ((), (), s32[]{:S(2)}) async-start(), calls=%async_computation.5 | async-start | bytes 3649536 | tf_op jit(solution)/shard_map/reduce_scatter | solution.py:325
  87.6 1.5 copy-start
  138.1 210.6 %reduce-scatter.3.cloned.1.call-start = ((), (), s32[]{:S(2)}) async-start(), calls=%async_computation.3 | async-start | bytes 3649536 | tf_op jit(solution)/shard_map/reduce_scatter | solution.py:325
  156.5 254.6 %all-gather.8.cloned.1.call-start = ((), (), s32[]{:S(2)}) async-start(), calls=%async_computation.6 | async-start | bytes 3649536 | tf_op jit(solution)/shard_map/all_gather | solution.py:329
  242.9 229.9 %all-gather.6.cloned.1.call-start = ((), (), s32[]{:S(2)}) async-start(), calls=%async_computation.4 | async-start | bytes 3649536 | tf_op jit(solution)/shard_map/all_gather | solution.py:329
Sparse Core Ops, SparseCore 0:
  10.5 36.6 all-gather.9
  138.2 103.0 reduce-scatter.4
  246.7 101.9 reduce-scatter.2
  352.1 59.0 all-gather.7
  413.9 58.8 all-gather.5
